TPU v7x, 32 devices: a whole 2x2x4 slice. The times are simulated.
32 devices in a mesh: grp: 2 (over y), run: 4 (over x, core), chan: 4 (over z).
Axes of the slice: x: 2, y: 2, z: 4, core: 2. Of those that a mesh axis runs over, the one named last changes fastest.
Arguments:
- embed: bfloat16 [512, 8192], P('grp', 'chan'), parts along dimension 0, may hold values from -6 to 6
- noise: bfloat16 [16, 32, 8192], P(('grp', 'run'), None, 'chan'), parts along dimension 0, may hold values from -12 to 12
- positions: int32 [16, 32], P(('grp', 'run')), parts along dimension 0, may hold values from 0 to 255
- restore: int32 [16, 2], P(('grp', 'run')), parts along dimension 0, may hold values 0 or 1
- short_one: float32 [7, 8192], P(None, 'chan'), may hold values from -2 to 2
- long_one: float32 [128, 8192], P(None, 'chan'), may hold values from -0.5 to 0.5
- out_weight: bfloat16 [8192, 8192], P(None, 'chan'), may hold values from -0.0625 to 0.0625
- short_two: float32 [7, 8192], P(None, 'chan'), may hold values from -2 to 2
- long_two: float32 [128, 8192], P(None, 'chan'), may hold values from -0.5 to 0.5
Outputs:
- traced: bfloat16 [16, 256, 8192], P(('grp', 'run'), None, 'chan'), parts along dimension 0
There are 2 independent parts, one for each index of `grp`. A program takes and returns all parts, laid end to end along the dimension named above; an argument that names none is the same for every part. Nothing has to cross between parts.
All inputs are finite; a program needn't handle non-finite values. No bound on the sum of `restore` on one device may be relied on, other than what follows from the above.
Results may differ from a plain program's by a relative error of at most 0.007.
Values may be sent and summed in bfloat16 or wider, within the bound.
A program may use at most 128 MiB of HBM per device.

v0:
```python
import jax
import jax.numpy as jnp
from jax import lax
from jax.sharding import PartitionSpec as P


def short_filter(field, filter_taps):
    length = field.shape[1]
    running = jnp.zeros(field.shape, jnp.float32)
    for shift_count in range(filter_taps.shape[0]):
        shifted = jnp.pad(field, ((0, 0), (shift_count, 0), (0, 0)))[:, :length]
        running = running + filter_taps[shift_count][None, None, :] * shifted
    return running


def block_filter(field, filter_taps):
    width = field.shape[2]
    span = filter_taps.shape[0]
    kernel = filter_taps[::-1][:, None, :]
    return lax.conv_general_dilated(
        field,
        kernel,
        window_strides=(1,),
        padding=((span - 1, 0),),
        dimension_numbers=("NWC", "WIO", "NWC"),
        feature_group_count=width,
        precision=lax.Precision.HIGHEST,
        preferred_element_type=jnp.float32,
    )


def per_device(
    embed, noise, positions, restore, short_one, long_one, out_weight, short_two, long_two
):
    run_count = noise.shape[0]
    length = embed.shape[0]
    first_run = lax.axis_index("run") * run_count
    run_ids = first_run + jnp.arange(run_count, dtype=jnp.int32)
    onehot = (jnp.arange(length, dtype=jnp.int32)[None, :, None] == positions[:, None, :]).astype(
        jnp.bfloat16
    )
    added = jnp.einsum("rlp,rpc->rlc", onehot, noise, preferred_element_type=jnp.float32)
    corrupt_flag = (run_ids != 0).astype(jnp.float32)[:, None, None]
    inputs = (embed.astype(jnp.float32)[None] + corrupt_flag * added).astype(jnp.bfloat16)
    batch_inputs = jnp.concatenate([inputs, embed[None]], axis=0)
    input_values = batch_inputs.astype(jnp.float32)
    filtered = block_filter(short_filter(input_values, short_one), long_one)
    mixed = (filtered * jax.nn.silu(input_values)).astype(jnp.bfloat16)
    initial = jnp.zeros((mixed.shape[0], length, out_weight.shape[1]), jnp.float32)
    segment = lax.all_gather(mixed, "chan", axis=2, tiled=True)
    weight_rows = lax.slice_in_dim(out_weight, 0, segment.shape[2], axis=0)
    projected = initial + jnp.einsum(
        "rlk,kc->rlc", segment, weight_rows, preferred_element_type=jnp.float32
    )
    hidden = (input_values + projected).astype(jnp.bfloat16)
    clean_hidden = hidden[run_count]
    hidden = hidden[:run_count]
    block_size = length // restore.shape[1]
    restored_rows = jnp.repeat(restore, block_size, axis=1)[:, :, None] == 1
    restored = jnp.where(restored_rows, clean_hidden[None], hidden)
    restored_values = restored.astype(jnp.float32)
    second = block_filter(short_filter(restored_values, short_two), long_two)
    return (restored_values + second * jax.nn.silu(restored_values)).astype(jnp.bfloat16)


def solution(mesh):
    in_specs = (
        P("grp", "chan"),
        P(("grp", "run"), None, "chan"),
        P(("grp", "run"), None),
        P(("grp", "run"), None),
        P(None, "chan"),
        P(None, "chan"),
        P(None, "chan"),
        P(None, "chan"),
        P(None, "chan"),
    )
    out_specs = P(("grp", "run"), None, "chan")
    return jax.shard_map(
        per_device, mesh=mesh, in_specs=in_specs, out_specs=out_specs, check_vma=False
    )
```

profile of v0, /device:TPU:0, one launch (start us, length us, event | category | flops | bytes accessed | tf_op | source)
XLA Modules:
  0.0 446.8 jit_solution(15623138889471099007)
XLA Ops:
  6.5 0.0 copy-start
  6.5 0.0 copy-start.6
  6.5 0.0 all-gather.2.cloned.1.call-start
  6.5 1.2 fusion.40
  7.8 0.0 copy-start.2
  7.8 2.9 convert_element_type.53
  10.7 8.9 %rev.6 = f32[128,2048]{1,0:T(8,128)} reverse(f32[128,2048]{1,0:T(8,128)} %param.14), dimensions={0} | reverse | bytes 2097152 | tf_op jit(solution)/shard_map/rev | solution.py:19
  19.5 0.0 copy-done
  19.5 0.0 copy-done.6
  19.5 2.4 add_convert_fusion.1
  22.0 0.0 copy-done.2
  22.0 0.4 maximum_convert_fusion
  22.4 0.0 copy-start.4
  22.4 5.2 %fusion.10 = f32[3,256,2048]{2,1,0:T(8,128)S(1)} fusion(f32[3,256,2048]{2,1,0:T(8,128)S(1)} %maximum_convert_fusion, f32[2048]{0:T(1024)S(1)} %bitcast.48, f32[2048]{0:T(1024)S(1)} %bitcast.49, f32[2048]{0:T(1024)S(1)} %bitcast.44, f32[2048]{0:T(1024)S(1)} %bitcast.45, f32[2048]{0:T(1024)S(1)} %bitcast.46, f32[2048]{0:T(1024)S(1)} %bitcast.47, ...), kind=kLoop, calls=%fused_computation.16 | loop fusion | flops 20447232 | bytes 12640256 | tf_op jit(solution)/shard_map/add | solution.py:12
  27.6 0.0 copy-done.4
  27.6 98.9 %fusion.2 = f32[3,256,2048]{2,0,1:T(4,128)S(1)} fusion(f32[3,256,2048]{2,1,0:T(8,128)S(1)} %fusion.10, f32[128,1,2048]{2,0,1:T(8,128)S(1)} %bitcast.35), kind=kOutput, calls=%fused_computation.2 | convolution fusion | flops 1816657920 | bytes 13631488 | tf_op jit(solution)/shard_map/conv_general_dilated | solution.py:20
  126.5 0.0 copy-start.7
  126.5 5.2 %fusion.16 = bf16[3,256,2048]{2,1,0:T(8,128)(2,1)} fusion(f32[3,256,2048]{2,0,1:T(4,128)S(1)} %fusion.2, bf16[1,256,2048]{2,1,0:T(8,128)(2,1)S(1)} %bitcast.32, bf16[2,256,2048]{2,1,0:T(8,128)(2,1)S(1)} %add_convert_fusion.1), kind=kLoop, calls=%fused_computation.23 | loop fusion | flops 12582912 | bytes 12582912 | tf_op jit(solution)/shard_map/convert_element_type | solution.py:48
  131.7 0.0 copy-start.5
  131.7 0.0 all-gather.2.cloned.1.call-update
  131.8 0.0 copy-done.7
  131.8 0.1 broadcast_bitcast_fusion
  131.9 8.9 %rev.7 = f32[128,2048]{1,0:T(8,128)} reverse(f32[128,2048]{1,0:T(8,128)} %param.17), dimensions={0} | reverse | bytes 2097152 | tf_op jit(solution)/shard_map/rev | solution.py:19
  140.7 0.0 copy-done.5
  140.8 212.0 %all-gather.2.cloned.1.call-done = bf16[3,256,8192]{2,1,0:T(8,128)(2,1)} async-done(((bf16[3,256,2048]{2,1,0:T(8,128)(2,1)}), bf16[3,256,8192]{2,1,0:T(8,128)(2,1)}) %all-gather.2.cloned.1.call-update) | async-done | bytes 12582928 | tf_op jit(solution)/shard_map/all_gather | solution.py:50
  352.8 33.6 %add_convert_fusion = bf16[3,256,2048]{2,1,0:T(8,128)(2,1)S(1)} fusion(bf16[3,256,8192]{2,1,0:T(8,128)(2,1)} %all-gather.2.cloned.1.call-done, bf16[8192,2048]{1,0:T(8,128)(2,1)} %param.15, bf16[1,256,2048]{2,1,0:T(8,128)(2,1)S(1)} %bitcast.33, bf16[2,256,2048]{2,1,0:T(8,128)(2,1)S(1)} %add_convert_fusion.1), kind=kOutput, calls=%fused_computation.24 | convolution fusion | flops 25776095232 | bytes 52428800 | tf_op jit(solution)/shard_map/rlk,kc->rlc/dot_general | solution.py:52
  386.5 0.1 slice_bitcast_fusion
  386.6 0.4 fusion.35
  386.9 0.0 copy-start.3
  386.9 3.5 fusion.23
  390.4 0.0 copy-done.3
  390.4 0.0 copy-start.1
  390.4 45.4 %fusion.31 = f32[2,256,2048]{2,0,1:T(2,128)S(1)} fusion(f32[2,256,2048]{2,1,0:T(8,128)S(1)} %fusion.23, f32[128,1,2048]{2,0,1:T(8,128)S(1)} %bitcast.34), kind=kOutput, calls=%fused_computation.46 | convolution fusion | flops 1211105280 | bytes 9437184 | tf_op jit(solution)/shard_map/conv_general_dilated | solution.py:20
  435.9 4.1 fusion.30
  439.9 0.0 copy-done.1
  (4 shorter events, 0.1 us)
Async XLA Ops:
  6.5 13.0 %copy-start = (bf16[2,32,2048]{2,1,0:T(8,128)(2,1)S(1)}, bf16[2,32,2048]{2,1,0:T(8,128)(2,1)}, u32[]{:S(2)}) copy-start(bf16[2,32,2048]{2,1,0:T(8,128)(2,1)} %param.10) | copy-start | bytes 786436
  6.5 13.0 %copy-start.6 = (s32[2,32]{1,0:T(2,128)S(1)}, s32[2,32]{1,0:T(2,128)}, u32[]{:S(2)}) copy-start(s32[2,32]{1,0:T(2,128)} %param.11) | copy-start | bytes 772
  6.5 346.3 %all-gather.2.cloned.1.call-start = ((), (), s32[]{:S(2)}) async-start(), calls=%async_computation | async-start | bytes 15728640 | tf_op jit(solution)/shard_map/all_gather | solution.py:50
  7.8 14.2 %copy-start.2 = (bf16[256,2048]{1,0:T(8,128)(2,1)S(1)}, bf16[256,2048]{1,0:T(8,128)(2,1)}, u32[]{:S(2)}) copy-start(bf16[256,2048]{1,0:T(8,128)(2,1)} %param.9) | copy-start | bytes 3145732
  22.4 5.2 %copy-start.4 = (f32[128,2048]{1,0:T(8,128)S(1)}, f32[128,2048]{1,0:T(8,128)}, u32[]{:S(2)}) copy-start(f32[128,2048]{1,0:T(8,128)} %rev.6) | copy-start | bytes 3145732
  126.5 5.3 %copy-start.7 = (s32[2,2]{1,0:T(2,128)S(1)}, s32[2,2]{1,0:T(2,128)}, u32[]{:S(2)}) copy-start(s32[2,2]{1,0:T(2,128)} %param.12) | copy-start | bytes 52
  131.7 9.0 %copy-start.5 = (f32[7,2048]{1,0:T(8,128)S(1)}, f32[7,2048]{1,0:T(8,128)}, u32[]{:S(2)}) copy-start(f32[7,2048]{1,0:T(8,128)} %param.16) | copy-start | bytes 172036
  386.9 3.5 copy-start.3
  390.4 49.5 %copy-start.1 = (bf16[2,32,2048]{2,1,0:T(8,128)(2,1)S(1)}, bf16[2,32,2048]{2,1,0:T(8,128)(2,1)}, u32[]{:S(2)}) copy-start(bf16[2,32,2048]{2,1,0:T(8,128)(2,1)} %param.10) | copy-start | bytes 786436
Sparse Core Ops, SparseCore 0:
  131.9 220.8 all-gather.1
where the time goes:
time: 448 us; the launch traced here: 447 us
  waiting for transfers between devices  212 us (47%)
  matrix products  180 us (40%)
  other arithmetic  21.6 us (5%)
  local copies, waits for them, and re-layouts  19.2 us (4%)
  between operations  13.6 us (3%)
    all_gather x1, waiting for transfers between devices, per_device(): segment = lax.all_gather(mixed, 'chan', axis=2, tiled=True)  212 us
    conv_general_dilated x2, matrix products, block_filter(): lax.conv_general_dilated(field, kernel, window_strides=(1,), padding=((sp...  144 us
    dot_general x1, matrix products, per_device(): jnp.einsum('rlk,kc->rlc', segment, weight_rows, preferred_element_type=jn...  33.6 us
    rev x2, local copies, waits for them, and re-layouts, block_filter(): kernel = filter_taps[::-1][:, None, :]  17.7 us
  transfers between devices with their start and end apart: 1, of which 1 were waited for; matrix products, arithmetic and copies ran while one was open for 2% of the time, Pallas kernels for 0%

commit v1 on v0

--- a/solution.py
+++ b/solution.py
@@ -47,7 +47,15 @@
     filtered = block_filter(short_filter(input_values, short_one), long_one)
     mixed = (filtered * jax.nn.silu(input_values)).astype(jnp.bfloat16)
     initial = jnp.zeros((mixed.shape[0], length, out_weight.shape[1]), jnp.float32)
-    segment = lax.all_gather(mixed, "chan", axis=2, tiled=True)
+    ways, here = (lax.axis_size("chan"), lax.axis_index("chan"))
+    grown, reach = (mixed, 1)
+    while reach < ways:
+        theirs = lax.ppermute(grown, "chan", [(d, d ^ reach) for d in range(ways)])
+        mine_first = jnp.concatenate([grown, theirs], axis=2)
+        theirs_first = jnp.concatenate([theirs, grown], axis=2)
+        grown = jnp.where(here & reach == 0, mine_first, theirs_first)
+        reach = 2 * reach
+    segment = grown
     weight_rows = lax.slice_in_dim(out_weight, 0, segment.shape[2], axis=0)
     projected = initial + jnp.einsum(
         "rlk,kc->rlc", segment, weight_rows, preferred_element_type=jnp.float32

time: 448 us -> 578 us (1.29)
  waiting for transfers between devices: 212 us -> 329 us
  between operations: 13.6 us -> 0.15 us
  other arithmetic: 21.6 us -> 33.4 us
  matrix products: 180 us -> 188 us
    ppermute x0 -> x2, waiting for transfers between devices: none -> 329 us  [per_device(): theirs = lax.ppermute(grown, 'chan', [(d, d ^ reach) for d in range(ways)])]
    all_gather x1 -> x0, waiting for transfers between devices: 212 us -> none  [per_device(): segment = lax.all_gather(mixed, 'chan', axis=2, tiled=True)]
    select_n x0 -> x1, other arithmetic: none -> 10.1 us  [per_device(): grown = jnp.where(here & reach == 0, mine_first, theirs_first)]
    dot_general x1, matrix products: 33.6 us -> 41.1 us  [per_device(): jnp.einsum('rlk,kc->rlc', segment, weight_rows, preferred_element_type=jn...]
    ppermute x0 -> x2, starting transfers between devices: none -> 5.78 us  [per_device(): theirs = lax.ppermute(grown, 'chan', [(d, d ^ reach) for d in range(ways)])]
  transfers between devices with their start and end apart: 1 -> 2, of which waited for: 1 -> 2; matrix products, arithmetic and copies ran while one was open for 2% -> 2% of each run, Pallas kernels for 0% -> 0%
where the time goes in v1:
time: 578 us; the launch traced here: 577 us
  waiting for transfers between devices  329 us (57%)
  matrix products  188 us (33%)
  other arithmetic  33.4 us (6%)
  local copies, waits for them, and re-layouts  20.4 us (4%)
  starting transfers between devices  5.78 us (1%)
    ppermute x2, waiting for transfers between devices, per_device(): theirs = lax.ppermute(grown, 'chan', [(d, d ^ reach) for d in range(ways)])  329 us
    conv_general_dilated x2, matrix products, block_filter(): lax.conv_general_dilated(field, kernel, window_strides=(1,), padding=((sp...  144 us
    dot_general x1, matrix products, per_device(): jnp.einsum('rlk,kc->rlc', segment, weight_rows, preferred_element_type=jn...  41.1 us
    rev x2, local copies, waits for them, and re-layouts, block_filter(): kernel = filter_taps[::-1][:, None, :]  17.7 us
  transfers between devices with their start and end apart: 2, of which 2 were waited for; matrix products, arithmetic and copies ran while one was open for 2% of the time, Pallas kernels for 0%

profile of v1, /device:TPU:0, one launch (start us, length us, event | category | flops | bytes accessed | tf_op | source)
XLA Modules:
  0.0 576.9 jit_solution(16836836126016092585)
XLA Ops:
  0.0 0.0 copy-start
  0.0 0.0 copy-start.2
  0.0 1.2 fusion.47
  1.2 2.8 convert_element_type.53
  4.0 8.9 %rev.6 = f32[128,2048]{1,0:T(8,128)} reverse(f32[128,2048]{1,0:T(8,128)} %param.14), dimensions={0} | reverse | bytes 2097152 | tf_op jit(solution)/shard_map/rev | solution.py:19
  12.9 0.0 copy-done
  12.9 2.4 add_convert_fusion.1
  15.4 0.0 copy-done.2
  15.4 0.4 maximum_convert_fusion
  15.8 0.0 copy-start.5
  15.8 5.2 fusion.16
  21.0 0.0 copy-done.5
  21.0 98.9 %fusion.8 = f32[3,256,2048]{2,0,1:T(4,128)S(1)} fusion(f32[3,256,2048]{2,1,0:T(8,128)S(1)} %fusion.16, f32[128,1,2048]{2,0,1:T(8,128)S(1)} %bitcast.34), kind=kOutput, calls=%fused_computation.9 | convolution fusion | flops 1816657920 | bytes 13631488 | tf_op jit(solution)/shard_map/conv_general_dilated | solution.py:20
  119.9 5.3 fusion.22
  125.2 3.0 collective-permute-start
  128.2 0.0 copy-start.7
  128.2 0.0 copy-start.6
  128.2 68.4 %collective-permute-done = bf16[3,256,2048]{2,1,0:T(8,128)(2,1)} collective-permute-done((bf16[3,256,2048]{2,1,0:T(8,128)(2,1)}, bf16[3,256,2048]{2,1,0:T(8,128)(2,1)}, u32[]{:S(2)}, u32[]{:S(2)}) %collective-permute-start) | collective-permute-done | bytes 3145760 | tf_op jit(solution)/shard_map/ppermute | solution.py:53
  196.6 10.1 %maximum_select_fusion.2 = bf16[3,256,4096]{2,1,0:T(8,128)(2,1)} fusion(bf16[3,256,2048]{2,1,0:T(8,128)(2,1)} %collective-permute-done, bf16[3,256,2048]{2,1,0:T(8,128)(2,1)} %fusion.22, pred[]{:T(512)S(6)} %eq.41), kind=kLoop, calls=%fused_computation.29 | loop fusion | flops 28311552 | bytes 12582913 | tf_op jit(solution)/shard_map/jit(_where)/select_n | solution.py:56
  206.7 2.8 collective-permute-start.1
  209.5 0.0 copy-done.7
  209.5 0.1 broadcast_bitcast_fusion
  209.6 8.9 %rev.7 = f32[128,2048]{1,0:T(8,128)} reverse(f32[128,2048]{1,0:T(8,128)} %param.17), dimensions={0} | reverse | bytes 2097152 | tf_op jit(solution)/shard_map/rev | solution.py:19
  218.4 0.0 copy-done.6
  218.5 261.0 %collective-permute-done.1 = bf16[3,256,4096]{2,1,0:T(8,128)(2,1)} collective-permute-done((bf16[3,256,4096]{2,1,0:T(8,128)(2,1)}, bf16[3,256,4096]{2,1,0:T(8,128)(2,1)}, u32[]{:S(2)}, u32[]{:S(2)}) %collective-permute-start.1) | collective-permute-done | bytes 6291488 | tf_op jit(solution)/shard_map/ppermute | solution.py:53
  479.4 41.1 %add_convert_fusion = bf16[3,256,2048]{2,1,0:T(8,128)(2,1)} fusion(bf16[8192,2048]{1,0:T(8,128)(2,1)} %param.15, bf16[3,256,4096]{2,1,0:T(8,128)(2,1)} %collective-permute-done.1, bf16[3,256,4096]{2,1,0:T(8,128)(2,1)} %maximum_select_fusion.2, pred[]{:T(512)S(6)} %eq.40, bf16[1,256,2048]{2,1,0:T(8,128)(2,1)S(1)} %bitcast.32, ...), kind=kOutput, calls=%fused_computation.32 | convolution fusion | flops 25832718336 | bytes 52428800 | tf_op jit(solution)/shard_map/rlk,kc->rlc/dot_general | solution.py:60
  520.5 1.3 slice_bitcast_fusion
  521.8 0.0 copy-start.4
  521.8 2.1 fusion.41
  523.9 3.5 fusion.29
  527.4 0.0 copy-done.4
  527.4 0.0 copy-start.3
  527.4 0.0 copy-start.1
  527.4 45.4 %fusion.37 = f32[2,256,2048]{2,0,1:T(2,128)S(1)} fusion(f32[2,256,2048]{2,1,0:T(8,128)S(1)} %fusion.29, f32[128,1,2048]{2,0,1:T(8,128)S(1)} %bitcast.33), kind=kOutput, calls=%fused_computation.54 | convolution fusion | flops 1211105280 | bytes 9437184 | tf_op jit(solution)/shard_map/conv_general_dilated | solution.py:20
  572.9 0.0 copy-done.3
  572.9 4.1 fusion.36
  576.9 0.0 copy-done.1
  (4 shorter events, 0.1 us)
Async XLA Ops:
  0.0 12.9 %copy-start = (bf16[2,32,2048]{2,1,0:T(8,128)(2,1)S(1)}, bf16[2,32,2048]{2,1,0:T(8,128)(2,1)}, u32[]{:S(2)}) copy-start(bf16[2,32,2048]{2,1,0:T(8,128)(2,1)} %param.10) | copy-start | bytes 786436
  0.0 15.4 %copy-start.2 = (bf16[256,2048]{1,0:T(8,128)(2,1)S(1)}, bf16[256,2048]{1,0:T(8,128)(2,1)}, u32[]{:S(2)}) copy-start(bf16[256,2048]{1,0:T(8,128)(2,1)} %param.9) | copy-start | bytes 3145732
  15.8 5.2 copy-start.5
  125.2 71.4 %collective-permute-start = (bf16[3,256,2048]{2,1,0:T(8,128)(2,1)}, bf16[3,256,2048]{2,1,0:T(8,128)(2,1)}, u32[]{:S(2)}, u32[]{:S(2)}) collective-permute-start(bf16[3,256,2048]{2,1,0:T(8,128)(2,1)} %fusion.22), channel_id=1, source_target_pairs={{0,1},{1,0},{2,3},{3,2},{4,5},{5,4},{6,7},{7,6},{8,9},{9,8},{10,11... | collective-permute-start | bytes 9437192 | tf_op jit(solution)/shard_map/ppermute | solution.py:53
  128.2 81.2 %copy-start.7 = (s32[2,2]{1,0:T(2,128)S(1)}, s32[2,2]{1,0:T(2,128)}, u32[]{:S(2)}) copy-start(s32[2,2]{1,0:T(2,128)} %param.12) | copy-start | bytes 52
  128.2 90.2 %copy-start.6 = (f32[7,2048]{1,0:T(8,128)S(1)}, f32[7,2048]{1,0:T(8,128)}, u32[]{:S(2)}) copy-start(f32[7,2048]{1,0:T(8,128)} %param.16) | copy-start | bytes 172036
  206.7 272.7 %collective-permute-start.1 = (bf16[3,256,4096]{2,1,0:T(8,128)(2,1)}, bf16[3,256,4096]{2,1,0:T(8,128)(2,1)}, u32[]{:S(2)}, u32[]{:S(2)}) collective-permute-start(bf16[3,256,4096]{2,1,0:T(8,128)(2,1)} %maximum_select_fusion.2), channel_id=1, source_target_pairs={{0,2},{1,3},{2,0},{3,1},{4,6},{5,7},{6,4},{7,5},{8,10},{9,11},{10,... | collective-permute-start | bytes 18874376 | tf_op jit(solution)/shard_map/ppermute | solution.py:53
  521.8 5.6 copy-start.4
  527.4 45.5 %copy-start.3 = (bf16[3,256,2048]{2,1,0:T(8,128)(2,1)S(1)}, bf16[3,256,2048]{2,1,0:T(8,128)(2,1)}, u32[]{:S(2)}) copy-start(bf16[3,256,2048]{2,1,0:T(8,128)(2,1)} %add_convert_fusion) | copy-start | bytes 9437188
  527.4 49.5 %copy-start.1 = (bf16[2,32,2048]{2,1,0:T(8,128)(2,1)S(1)}, bf16[2,32,2048]{2,1,0:T(8,128)(2,1)}, u32[]{:S(2)}) copy-start(bf16[2,32,2048]{2,1,0:T(8,128)(2,1)} %param.10) | copy-start | bytes 786436
